TPU v7x, 32 devices: a whole 2x2x4 slice. The times are simulated.
32 devices in a mesh: cent: 8 (over z, y), grp: 4 (over x, core).
Axes of the slice: x: 2, y: 2, z: 4, core: 2. Of those that a mesh axis runs over, the one named last changes fastest.
Arguments:
- queries: bfloat16 [64, 32, 128], P('grp'), may hold values from -6 to 6
- centroids: bfloat16 [262144, 128], P('cent'), may hold values from -0.5 to 0.5
- candidates: int32 [4, 8, 2, 64], P('grp', 'cent'), may hold values from 0 to 16383, as said below
- token_codes: int32 [16384, 128], P(('cent', 'grp')), may hold values from 0 to 32767
- resid_words: int32 [16384, 32, 128], P(('cent', 'grp')), may hold values from 0 to 255
- lengths: int32 [16384], P(('cent', 'grp')), may hold values from 1 to 128
- levels: float32 [4, 128], replicated, may hold values from -0.3125 to 0.3125
Outputs:
- token_best: float32 [64, 32], P('grp')
- passage_scores: float32 [4, 8, 2, 64], P('grp', 'cent')
Inputs may be any that keep to these rules, and one draw needn't show every extreme that they name: `candidates`: the entries of one [g, c] block are all different and name at most 8 passages of any one owner block (passages owner * 512 to owner * 512 + 511); one owner block gets exactly 8 from every [g, c] block.
All inputs are finite; a program needn't handle non-finite values.
Results may differ from a plain program's by a relative error of at most 0.0003.
Values may be sent and summed in bfloat16 or wider, within the bound.
No kernel may reach another device: no remote copies, remote signals or barrier semaphores. Data moves between devices by JAX's collectives and lax.ppermute only.
A program may use at most 128 MiB of HBM per device.

v0:
```python
import functools

import jax
import jax.numpy as jnp
from jax import lax
from jax.experimental import pallas as pl
from jax.experimental.pallas import tpu as pltpu
from jax.sharding import PartitionSpec as P

MASKED = -1000000000.0
LANES = 128
SUB = 8
FIELDS = 4
BLOCKS = 16
ALIGN = 8
TILE = 1024
MIB = 1 << 20


def transposed_by_eye(row):
    size = row.shape[1]
    down = lax.broadcasted_iota(jnp.int32, (size, size), 0)
    across = lax.broadcasted_iota(jnp.int32, (size, size), 1)
    return jnp.sum(jnp.where(down == across, row, 0.0), axis=1, keepdims=True)


def one_row(rows):
    return jnp.concatenate([rows[index : index + 1, :] for index in range(rows.shape[0])], axis=1)


def ids_kernel(cand_ref, ids_ref):
    ids_ref[...] = jnp.broadcast_to(one_row(cand_ref[...]), ids_ref.shape)


def ids_for_all(cand, devices):
    vmem = pl.BlockSpec(memory_space=pltpu.VMEM)
    return pl.pallas_call(
        ids_kernel,
        in_specs=[vmem],
        out_specs=vmem,
        out_shape=jax.ShapeDtypeStruct((devices, cand.size), jnp.int32),
        name="ids_for_all",
    )(cand)


def score_kernel(
    sizes,
    me_ref,
    cand_ref,
    own_ref,
    levels_ref,
    cent_hbm,
    words_hbm,
    codes_hbm,
    lens_hbm,
    *rest,
):
    group_count, cent_count, per_device, query_len, capacity, pass_dev, cand_count = sizes
    query_hbm = rest[:group_count]
    (
        out_ref, staged, table, words, query_rows, query_t, own_t, dense, embed, maxima, ids_vmem, ids, codes, lens,
        work, work_quad, item_pass, item_len, item_lane, table_sem, words_sem, query_sem, small_sem,
    ) = rest[group_count:]
    sources = cand_ref.shape[0]
    pairs = per_device * cand_count
    items = sources * capacity
    tiles = words.shape[1] // SUB
    tile_tokens = SUB * FIELDS
    quad_sources = LANES // (per_device * query_len)
    quads = sources // quad_sources
    group_quads = cent_count // quad_sources
    per_bits = per_device.bit_length() - 1
    tile_bits = tiles.bit_length() - 1
    part_rows = staged.shape[0] // quads
    word_parts = words_sem.shape[0]
    part_pass = pass_dev // word_parts

    def table_copy(part):
        rows = pl.ds(pl.multiple_of(part * part_rows, part_rows), part_rows)
        return pltpu.make_async_copy(cent_hbm.at[rows, :], staged.at[rows, :], table_sem.at[part])

    def words_copy(part):
        rows = pl.ds(part * part_pass, part_pass)
        return pltpu.make_async_copy(words_hbm.at[rows], words.at[rows], words_sem.at[part])

    def start_table(part, carry):
        table_copy(part).start()
        return carry

    group = jnp.bitwise_and(me_ref[0], group_count - 1)

    def query_copy(apart):
        return pltpu.make_async_copy(
            query_hbm[apart], query_rows.at[jnp.bitwise_xor(group, apart)], query_sem.at[apart]
        )

    lens_copy = pltpu.make_async_copy(lens_hbm, lens, small_sem.at[0])
    codes_copy = pltpu.make_async_copy(codes_hbm, codes, small_sem.at[1])
    lens_copy.start()
    for apart in range(group_count):
        query_copy(apart).start()
    lax.fori_loop(0, quads, start_table, 0)
    codes_copy.start()
    for part in range(word_parts):
        words_copy(part).start()

    first = me_ref[0] * pass_dev
    local = cand_ref[...] - first
    mine = (local >= 0) & (local < pass_dev)
    earlier = lax.broadcasted_iota(jnp.int32, (pairs, pairs), 0) < lax.broadcasted_iota(
        jnp.int32, (pairs, pairs), 1
    )
    slots = jnp.dot(
        mine.astype(jnp.bfloat16), earlier.astype(jnp.bfloat16), preferred_element_type=jnp.float32
    )
    which = lax.broadcasted_iota(jnp.int32, local.shape, 1) >= cand_count
    tagged = (local * per_device + which.astype(jnp.int32) + 1).astype(jnp.float32)
    lane = lax.broadcasted_iota(jnp.int32, ids_vmem.shape, 1)
    found = jnp.zeros(ids_vmem.shape, jnp.float32)
    for slot in range(capacity):
        chosen = jnp.sum(jnp.where(mine & (slots == slot), tagged, 0.0), axis=1, keepdims=True)
        found = jnp.where(lane == slot, chosen, found)
    ids_vmem[...] = found.astype(jnp.int32)
    ids_copy = pltpu.make_async_copy(ids_vmem, ids, small_sem.at[2])
    ids_copy.start()

    maxima[...] = jnp.full(maxima.shape, MASKED, jnp.float32)
    own_t[...] = jnp.transpose(own_ref[...].astype(jnp.float32)).astype(jnp.bfloat16)
    lens_copy.wait()
    ids_copy.wait()
    for apart in range(group_count):
        query_copy(apart).wait()

    item_pass[items] = 0
    item_len[items] = 0
    item_lane[items] = -1
    spare = items * tiles

    def prepare(quad, count):
        table_copy(quad).wait()
        rows = pl.ds(pl.multiple_of(quad * part_rows, part_rows), part_rows)
        table[rows, :] = staged[rows, :].astype(jnp.float32)
        block = query_rows[quad // group_quads, pl.ds(quad % group_quads * LANES, LANES), :]
        query_t[quad] = jnp.transpose(block.astype(jnp.float32)).astype(jnp.bfloat16)
        start = count
        for part in range(quad_sources):
            cent = quad % group_quads * quad_sources + part
            source = cent * group_count + quad // group_quads
            for slot in range(capacity):
                tag = ids[source, slot] - 1
                item = source * capacity + slot
                real = tag >= 0
                held = jnp.maximum(tag, 0)
                passage = jnp.right_shift(held, per_bits)
                length = lens[passage]
                item_pass[item] = passage
                item_len[item] = length
                item_lane[item] = part * per_device + jnp.bitwise_and(held, per_device - 1)
                for tile in range(tiles):
                    work[count + tile] = item * tiles + tile
                count = count + jnp.where(real, jnp.right_shift(length + tile_tokens - 1, tile_tokens.bit_length() - 1), 0)
        for index in range(ALIGN):
            work[count + index] = spare
        count = (count + ALIGN - 1) // ALIGN * ALIGN
        for index in range(quad_sources * capacity * tiles // ALIGN):
            work_quad[start // ALIGN + index] = quad
        return count

    total = lax.fori_loop(0, quads, prepare, 0)
    for index in range(2 * BLOCKS):
        work[total + index] = spare
    for index in range(2 * BLOCKS // ALIGN):
        work_quad[total // ALIGN + index] = 0
    chunks = jnp.maximum((total + BLOCKS - 1) // BLOCKS, 2)
    codes_copy.wait()
    for part in range(word_parts):
        words_copy(part).wait()

    sub = lax.broadcasted_iota(jnp.int32, (SUB, LANES), 0)
    position = jnp.concatenate([sub * FIELDS + field for field in range(FIELDS)], axis=0)
    lane_group = lax.broadcasted_iota(jnp.int32, (1, LANES), 1) // query_len
    level = [levels_ref[index : index + 1, :] for index in range(FIELDS)]

    def score(chunk):
        scores = []
        for part in range(BLOCKS // ALIGN):
            rows = embed[part * ALIGN * tile_tokens : (part + 1) * ALIGN * tile_tokens, :]
            quad = work_quad[chunk * (BLOCKS // ALIGN) + part]
            scores.append(jnp.dot(rows, query_t[quad], preferred_element_type=jnp.float32))
        for index in range(BLOCKS):
            entry = work[chunk * BLOCKS + index]
            item, tile = jnp.right_shift(entry, tile_bits), jnp.bitwise_and(entry, tiles - 1)
            inner = index % ALIGN
            block = scores[index // ALIGN][inner * tile_tokens : (inner + 1) * tile_tokens]
            kept = jnp.where(position < item_len[item] - tile * tile_tokens, block, MASKED)
            best = jnp.max(kept, axis=0, keepdims=True)
            maxima[tile, pl.ds(item, 1), :] = jnp.where(lane_group == item_lane[item], best, 0.0)

    def decode(chunk):
        for index in range(BLOCKS):
            entry = work[chunk * BLOCKS + index]
            item, tile = jnp.right_shift(entry, tile_bits), jnp.bitwise_and(entry, tiles - 1)
            passage = item_pass[item]
            start = passage * (tiles * tile_tokens) + tile * tile_tokens
            word = words[passage, pl.ds(pl.multiple_of(tile * SUB, SUB), SUB), :]
            for field in range(FIELDS):
                rows = jnp.zeros((SUB, LANES), jnp.float32)
                for row in range(SUB):
                    code = codes[start + (row * FIELDS + field)]
                    rows = jnp.where(sub == row, table[pl.ds(code, SUB, stride=0), :], rows)
                low = jnp.bitwise_and(word, 1 << (2 * field)) != 0
                high = jnp.bitwise_and(word, 2 << (2 * field)) != 0
                residual = jnp.where(
                    high, jnp.where(low, level[3], level[2]), jnp.where(low, level[1], level[0])
                )
                base = index * tile_tokens + field * SUB
                dense[base : base + SUB, :] = rows + residual

    def normalize():
        for index in range(BLOCKS):
            rows = slice(index * tile_tokens, (index + 1) * tile_tokens)
            block = dense[rows, :]
            inverse = lax.rsqrt(jnp.sum(block * block, axis=1, keepdims=True) + 1e-06)
            embed[rows, :] = (block * inverse).astype(jnp.bfloat16)

    tile_rows = min(staged.shape[0], TILE)
    best_tiles = staged.shape[0] // tile_rows

    def centroid_tile(index, best):
        block = staged[pl.ds(pl.multiple_of(index * tile_rows, tile_rows), tile_rows), :]
        scores = jnp.dot(block, own_t[...], preferred_element_type=jnp.float32)
        return jnp.maximum(best, jnp.max(scores.reshape(tile_rows // SUB, SUB, scores.shape[1]), axis=0))

    decode(0)
    normalize()
    decode(1)

    def step(chunk, carry):
        score(chunk - 2)
        normalize()
        decode(chunk)
        return carry

    def step_with_tile(chunk, best):
        step(chunk, 0)
        return centroid_tile(chunk - 2, best)

    token_best = jnp.full((SUB, own_t.shape[1]), -jnp.inf, jnp.float32)
    shared = jnp.minimum(chunks, best_tiles + 2)
    token_best = lax.fori_loop(2, shared, step_with_tile, token_best)
    lax.fori_loop(shared, chunks, step, 0)
    score(chunks - 2)
    normalize()
    score(chunks - 1)
    token_best = lax.fori_loop(shared - 2, best_tiles, centroid_tile, token_best)
    token_best = jnp.max(token_best, axis=0, keepdims=True)

    best = maxima[0, :items, :]
    for tile in range(1, tiles):
        best = jnp.maximum(best, maxima[tile, :items, :])
    sums = jnp.sum(best, axis=1, keepdims=True) / query_len
    item_down = lax.broadcasted_iota(jnp.int32, (items, LANES), 0)
    item_slot = lax.broadcasted_iota(jnp.int32, (items, LANES), 1)
    spread = jnp.where(item_down % capacity == item_slot, sums, 0.0)
    source_down = lax.broadcasted_iota(jnp.int32, (sources, items), 0)
    item_across = lax.broadcasted_iota(jnp.int32, (sources, items), 1)
    gather = (item_across // capacity == source_down).astype(jnp.float32)
    by_source = jnp.dot(
        gather, spread, precision=lax.Precision.HIGHEST, preferred_element_type=jnp.float32
    )
    best_lanes = token_best.shape[1]
    for source in range(sources):
        out_ref[source, :, :best_lanes] = token_best
        out_ref[source, :, best_lanes:] = by_source[source : source + 1, :]


def owner_scores(me, cand_all, query_parts, centroids, token_codes, resid_words, lengths, levels, sizes):
    capacity = sizes[4]
    sources = cand_all.shape[0]
    group_count = len(query_parts)
    group_rows = query_parts[0].shape[0]
    cent_dev, width = centroids.shape
    pass_dev, plen = token_codes.shape
    packed = resid_words.shape[1]
    tiles = packed // SUB
    items = sources * capacity
    quads = group_count * group_rows // LANES
    work_size = items * tiles + quads * ALIGN + 2 * BLOCKS
    any_space = pl.BlockSpec(memory_space=pl.ANY)
    vmem = pl.BlockSpec(memory_space=pltpu.VMEM)
    tokens = items * plen
    return pl.pallas_call(
        functools.partial(score_kernel, sizes),
        in_specs=[pl.BlockSpec(memory_space=pltpu.SMEM), vmem, vmem, vmem] + [any_space] * (4 + group_count),
        out_specs=vmem,
        out_shape=jax.ShapeDtypeStruct((sources, 1, group_rows + LANES), jnp.float32),
        scratch_shapes=[
            pltpu.VMEM((cent_dev, width), jnp.bfloat16),
            pltpu.VMEM((cent_dev + SUB, width), jnp.float32),
            pltpu.VMEM((pass_dev, packed, width), jnp.int32),
            pltpu.VMEM((group_count, group_rows, width), jnp.bfloat16),
            pltpu.VMEM((quads, width, LANES), jnp.bfloat16),
            pltpu.VMEM((width, group_rows), jnp.bfloat16),
            pltpu.VMEM((BLOCKS * SUB * FIELDS, width), jnp.float32),
            pltpu.VMEM((BLOCKS * SUB * FIELDS, width), jnp.bfloat16),
            pltpu.VMEM((tiles, items + SUB, LANES), jnp.float32),
            pltpu.VMEM((sources, LANES), jnp.int32),
            pltpu.SMEM((sources, LANES), jnp.int32),
            pltpu.SMEM((pass_dev * plen,), jnp.int32),
            pltpu.SMEM((pass_dev,), jnp.int32),
            pltpu.SMEM((work_size,), jnp.int32),
            pltpu.SMEM((work_size // ALIGN + items * tiles // quads,), jnp.int32),
            pltpu.SMEM((items + 1,), jnp.int32),
            pltpu.SMEM((items + 1,), jnp.int32),
            pltpu.SMEM((items + 1,), jnp.int32),
            pltpu.SemaphoreType.DMA((quads,)),
            pltpu.SemaphoreType.DMA((4,)),
            pltpu.SemaphoreType.DMA((group_count,)),
            pltpu.SemaphoreType.DMA((3,)),
        ],
        compiler_params=pltpu.CompilerParams(vmem_limit_bytes=56 * MIB),
        cost_estimate=pl.CostEstimate(
            flops=2 * (tokens * LANES + cent_dev * group_rows) * width, bytes_accessed=2 * cent_dev * width * 2, transcendentals=tokens
        ),
        name="owner_scores",
    )(
        me, cand_all, query_parts[0], levels, centroids, resid_words, token_codes.reshape(pass_dev * plen), lengths, *query_parts
    )


def finish_kernel(sizes, me_ref, back_ref, cand_ref, best_out, score_out):
    group_count, cent_count, _, query_len, capacity, pass_dev, _ = sizes
    group = jnp.bitwise_and(me_ref[0], group_count - 1)
    best_lanes = best_out.shape[0] * query_len
    best = back_ref[group, :, :best_lanes]
    for cent in range(1, cent_count):
        best = jnp.maximum(best, back_ref[cent * group_count + group, :, :best_lanes])
    for index in range(best_out.shape[0]):
        best_out[index : index + 1, :] = best[:, index * query_len : (index + 1) * query_len]
    back = back_ref[:, 0, best_lanes:]
    owners = jnp.right_shift(one_row(cand_ref[...]), pass_dev.bit_length() - 1).astype(jnp.float32)
    pairs = owners.shape[1]
    earlier = lax.broadcasted_iota(jnp.int32, (pairs, pairs), 0) < lax.broadcasted_iota(
        jnp.int32, (pairs, pairs), 1
    )
    same = transposed_by_eye(owners) == owners
    slots = jnp.sum(jnp.where(same & earlier, 1.0, 0.0), axis=0, keepdims=True)
    target = (owners * capacity + slots).astype(jnp.int32)
    owner = lax.broadcasted_iota(jnp.int32, (back.shape[0], pairs), 0)
    found = jnp.zeros(owner.shape, jnp.float32)
    for slot in range(capacity):
        found = found + jnp.where(owner * capacity + slot == target, back[:, slot : slot + 1], 0.0)
    scores = jnp.sum(found, axis=0, keepdims=True)
    width = score_out.shape[1]
    for index in range(score_out.shape[0]):
        score_out[index : index + 1, :] = scores[:, index * width : (index + 1) * width]


def finish(me, back, cand, group_rows, sizes):
    _, _, per_device, query_len, _, _, cand_count = sizes
    vmem = pl.BlockSpec(memory_space=pltpu.VMEM)
    return pl.pallas_call(
        functools.partial(finish_kernel, sizes),
        in_specs=[pl.BlockSpec(memory_space=pltpu.SMEM), vmem, vmem],
        out_specs=[vmem] * 2,
        out_shape=[
            jax.ShapeDtypeStruct((group_rows, query_len), jnp.float32),
            jax.ShapeDtypeStruct((per_device, cand_count), jnp.float32),
        ],
        name="finish",
    )(me, back, cand)


def shards(queries, centroids, candidates, token_codes, resid_words, lengths, levels):
    group_rows, query_len, width = queries.shape
    pass_dev = token_codes.shape[0]
    per_device, cand_count = candidates.shape[2:]
    pair_count = per_device * cand_count
    cent_count = lax.axis_size("cent")
    group_count = lax.axis_size("grp")
    devices = cent_count * group_count
    capacity = max(2, 2 * pair_count // devices)
    sizes = (group_count, cent_count, per_device, query_len, capacity, pass_dev, cand_count)
    cand = candidates.reshape(per_device, cand_count)
    query_rows = queries.reshape(group_rows * query_len, width)
    me = (lax.axis_index("cent") * group_count + lax.axis_index("grp")).astype(jnp.int32).reshape(1)
    cand_all = lax.all_to_all(
        ids_for_all(cand, devices), ("cent", "grp"), split_axis=0, concat_axis=0, tiled=True
    )
    query_parts = [query_rows]
    for apart in range(1, group_count):
        pairs = [(index, index ^ apart) for index in range(group_count)]
        query_parts.append(lax.ppermute(query_rows, "grp", pairs))
    reply = owner_scores(
        me, cand_all, query_parts, centroids, token_codes, resid_words, lengths, levels, sizes
    )
    back = lax.all_to_all(reply, ("cent", "grp"), split_axis=0, concat_axis=0, tiled=True)
    token_best, scores = finish(me, back, cand, group_rows, sizes)
    return (token_best, scores.reshape(1, 1, per_device, cand_count))


def solution(mesh):
    placed = (
        P("grp", None, None),
        P("cent", None),
        P("grp", "cent", None, None),
        P(("cent", "grp"), None),
        P(("cent", "grp"), None, None),
        P(("cent", "grp")),
        P(),
    )
    return jax.shard_map(
        shards,
        mesh=mesh,
        in_specs=placed,
        out_specs=(P("grp", None), P("grp", "cent", None, None)),
        check_vma=False,
    )
```

profile of v0, /device:TPU:0, one launch (start us, length us, event | category | flops | bytes accessed | tf_op | source)
XLA Modules:
  0.0 68.1 jit_solution(12986774815007452704)
XLA Ops:
  0.6 2.4 %collective-permute-start.2 = (bf16[512,128]{1,0:T(8,128)(2,1)}, bf16[512,128]{1,0:T(8,128)(2,1)S(1)}, u32[]{:S(2)}, u32[]{:S(2)}) collective-permute-start(bf16[512,128]{1,0:T(8,128)(2,1)} %bitcast.14), channel_id=1, source_target_pairs={{0,3},{1,2},{2,1},{3,0},{4,7},{5,6},{6,5},{7,4},{8,11},{9,10},{10,... | collective-permute-start | bytes 393224 | tf_op jit(solution)/shard_map/ppermute | solution.py:393
  3.1 0.6 collective-permute-start.1
  3.7 0.0 collective-permute-start
  3.8 1.3 %ids_for_all.1 = s32[32,128]{1,0:T(8,128)} custom-call(s32[2,64]{1,0:T(2,128)} %bitcast.11), custom_call_target="tpu_custom_call" | custom-call | tf_op jit(solution)/shard_map/ids_for_all/pallas_call | solution.py:37
  5.1 6.1 %all-to-all-start = ((s32[32,1,128]{2,1,0:T(1,128)}), s32[32,1,128]{2,1,0:T(1,128)S(1)}, u32[]{:S(2)}, u32[]{:S(2)}) async-start(s32[32,1,128]{2,1,0:T(1,128)} %bitcast.9), calls=%async_computation | async-start | bytes 32768 | tf_op jit(solution)/shard_map/all_to_all | solution.py:387
  11.2 7.1 %all-to-all-done = s32[32,1,128]{2,1,0:T(1,128)S(1)} async-done(((s32[32,1,128]{2,1,0:T(1,128)}), s32[32,1,128]{2,1,0:T(1,128)S(1)}, u32[]{:S(2)}, u32[]{:S(2)}) %all-to-all-start) | async-done | bytes 16416 | tf_op jit(solution)/shard_map/all_to_all | solution.py:387
  18.4 0.0 copy-start
  18.4 0.0 collective-permute-done.2.rest_3_
  18.4 0.0 copy-start.1
  18.4 0.0 collective-permute-done.1.rest_2_
  18.4 0.0 copy-start.2
  18.4 0.0 collective-permute-done.rest_1_
  18.4 0.0 copy-start.3
  18.4 0.6 copy-done
  18.9 0.1 copy-done.1
  19.0 0.1 copy-done.2
  19.1 0.0 copy-done.3
  19.1 35.9 %owner_scores.1 = f32[32,1,640]{2,1,0:T(1,128)} custom-call(s32[1]{0:T(128)} %bitcast.me_ref, s32[32,128]{1,0:T(8,128)} %bitcast.10, bf16[512,128]{1,0:T(8,128)(2,1)} %bitcast.17, f32[4,128]{1,0:T(4,128)} %levels_ref.1, bf16[32768,128]{1,0:T(8,128)(2,1)} %cent_hbm.1, s32[512,32,128]{2,1,0:T(8,128)} %words_hbm.1, s32[65536]{0:T(1024)} %bitcast.13, ...), custom_call_target="tpu_custom_call" | custom-call | flops 5368709120 | bytes 16777216 | tf_op jit(solution)/shard_map/owner_scores/pallas_call | solution.py:292
  55.0 11.1 %all_to_all.16.back_ref = f32[32,1,640]{2,1,0:T(1,128)} all-to-all(f32[32,1,640]{2,1,0:T(1,128)} %owner_scores.1), channel_id=1, replica_groups=mesh['cent'=8,'grp'=4] {'cent','grp'}, dimensions={0} | all-to-all | bytes 163840 | tf_op jit(solution)/shard_map/all_to_all | solution.py:397
  66.1 2.0 %finish.1 = (f32[16,32]{1,0:T(8,128)}, f32[2,64]{1,0:T(2,128)}) custom-call(s32[1]{0:T(128)} %bitcast.me_ref, f32[32,1,640]{2,1,0:T(1,128)} %all_to_all.16.back_ref, s32[2,64]{1,0:T(2,128)} %bitcast.12), custom_call_target="tpu_custom_call" | custom-call | tf_op jit(solution)/shard_map/finish/pallas_call | solution.py:362
Async XLA Ops:
  0.6 17.7 %collective-permute-start.2 = (bf16[512,128]{1,0:T(8,128)(2,1)}, bf16[512,128]{1,0:T(8,128)(2,1)S(1)}, u32[]{:S(2)}, u32[]{:S(2)}) collective-permute-start(bf16[512,128]{1,0:T(8,128)(2,1)} %bitcast.14), channel_id=1, source_target_pairs={{0,3},{1,2},{2,1},{3,0},{4,7},{5,6},{6,5},{7,4},{8,11},{9,10},{10,... | collective-permute-start | bytes 393224 | tf_op jit(solution)/shard_map/ppermute | solution.py:393
  3.1 15.3 %collective-permute-start.1 = (bf16[512,128]{1,0:T(8,128)(2,1)}, bf16[512,128]{1,0:T(8,128)(2,1)S(1)}, u32[]{:S(2)}, u32[]{:S(2)}) collective-permute-start(bf16[512,128]{1,0:T(8,128)(2,1)} %bitcast.15), channel_id=1, source_target_pairs={{0,2},{1,3},{2,0},{3,1},{4,6},{5,7},{6,4},{7,5},{8,10},{9,11},{10,... | collective-permute-start | bytes 393224 | tf_op jit(solution)/shard_map/ppermute | solution.py:393
  3.7 14.7 %collective-permute-start = (bf16[512,128]{1,0:T(8,128)(2,1)}, bf16[512,128]{1,0:T(8,128)(2,1)S(1)}, u32[]{:S(2)}, u32[]{:S(2)}) collective-permute-start(bf16[512,128]{1,0:T(8,128)(2,1)} %bitcast.16), channel_id=1, source_target_pairs={{0,1},{1,0},{2,3},{3,2},{4,5},{5,4},{6,7},{7,6},{8,9},{9,8},{10,11... | collective-permute-start | bytes 393224 | tf_op jit(solution)/shard_map/ppermute | solution.py:393
  5.1 13.3 %all-to-all-start = ((s32[32,1,128]{2,1,0:T(1,128)}), s32[32,1,128]{2,1,0:T(1,128)S(1)}, u32[]{:S(2)}, u32[]{:S(2)}) async-start(s32[32,1,128]{2,1,0:T(1,128)} %bitcast.9), calls=%async_computation | async-start | bytes 32768 | tf_op jit(solution)/shard_map/all_to_all | solution.py:387
  18.4 0.6 copy-start
  18.4 0.6 copy-start.1
  18.4 0.7 %copy-start.2 = (bf16[512,128]{1,0:T(8,128)(2,1)}, bf16[512,128]{1,0:T(8,128)(2,1)S(1)}, u32[]{:S(2)}) copy-start(bf16[512,128]{1,0:T(8,128)(2,1)S(1)} %collective-permute-done.1.rest_2_) | copy-start | bytes 393220
  18.4 0.7 %copy-start.3 = (bf16[512,128]{1,0:T(8,128)(2,1)}, bf16[512,128]{1,0:T(8,128)(2,1)S(1)}, u32[]{:S(2)}) copy-start(bf16[512,128]{1,0:T(8,128)(2,1)S(1)} %collective-permute-done.rest_1_) | copy-start | bytes 393220
where the time goes:
time: 68.4 us; the launch traced here: 68.1 us
  Pallas kernels  39.2 us (57%)
  blocking collectives  11.1 us (16%)
  starting transfers between devices  9.22 us (13%)
  waiting for transfers between devices  7.15 us (10%)
  local copies, waits for them, and re-layouts  0.7 us (1%)
  between operations  0.69 us (1%)
    pallas_call x1, Pallas kernels, owner_scores(): pl.pallas_call(functools.partial(score_kernel, sizes), in_specs=[pl.Block...  35.9 us
    all_to_all x1, blocking collectives, shards(): lax.all_to_all(reply, ('cent', 'grp'), split_axis=0, concat_axis=0, tiled...  11.1 us
    all_to_all x1, waiting for transfers between devices, shards(): lax.all_to_all(ids_for_all(cand, devices), ('cent', 'grp'), split_axis=0,...  7.14 us
    all_to_all x1, starting transfers between devices, shards(): lax.all_to_all(ids_for_all(cand, devices), ('cent', 'grp'), split_axis=0,...  6.1 us
    ppermute x3, starting transfers between devices, shards(): query_parts.append(lax.ppermute(query_rows, 'grp', pairs))  3.12 us
    pallas_call x1, Pallas kernels, finish(): pl.pallas_call(functools.partial(finish_kernel, sizes), in_specs=[pl.Bloc...  1.97 us
  transfers between devices with their start and end apart: 4, of which 1 were waited for; matrix products, arithmetic and copies ran while one was open for 0% of the time, Pallas kernels for 2%

commit v1 on v0

--- a/solution.py
+++ b/solution.py
@@ -14,6 +14,8 @@
 BLOCKS = 16
 ALIGN = 8
 TILE = 1024
+PARTS = 16
+WORD_PARTS = 4
 MIB = 1 << 20
 
 
@@ -43,14 +45,66 @@
     )(cand)
 
 
+def tables_kernel(cent_hbm, words_hbm, table, staged, words, table_sem, words_sem):
+    rows = staged.shape[0] // PARTS
+    word_rows = words.shape[0] // WORD_PARTS
+
+    def table_copy(part):
+        piece = pl.ds(pl.multiple_of(part * rows, rows), rows)
+        return pltpu.make_async_copy(cent_hbm.at[piece, :], staged.at[piece, :], table_sem.at[part])
+
+    def words_copy(part):
+        piece = pl.ds(part * word_rows, word_rows)
+        return pltpu.make_async_copy(words_hbm.at[piece], words.at[piece], words_sem.at[part])
+
+    for part in range(PARTS):
+        table_copy(part).start()
+    for part in range(WORD_PARTS):
+        words_copy(part).start()
+
+    def widen(part, carry):
+        table_copy(part).wait()
+        piece = pl.ds(pl.multiple_of(part * rows, rows), rows)
+        table[piece, :] = staged[piece, :].astype(jnp.float32)
+        return carry
+
+    lax.fori_loop(0, PARTS, widen, 0)
+    for part in range(WORD_PARTS):
+        words_copy(part).wait()
+
+
+def tables(centroids, resid_words):
+    cent_dev, width = centroids.shape
+    vmem = pl.BlockSpec(memory_space=pltpu.VMEM)
+    centroids = pltpu.with_memory_space_constraint(centroids, pltpu.HBM)
+    resid_words = pltpu.with_memory_space_constraint(resid_words, pltpu.HBM)
+    return pl.pallas_call(
+        tables_kernel,
+        in_specs=[pl.BlockSpec(memory_space=pltpu.HBM)] * 2,
+        out_specs=[vmem] * 3,
+        out_shape=[
+            pltpu.VMEM((cent_dev + SUB, width), jnp.float32),
+            pltpu.VMEM((cent_dev, width), jnp.bfloat16),
+            pltpu.VMEM(resid_words.shape, jnp.int32),
+        ],
+        scratch_shapes=[pltpu.SemaphoreType.DMA((PARTS,)), pltpu.SemaphoreType.DMA((WORD_PARTS,))],
+        compiler_params=pltpu.CompilerParams(vmem_limit_bytes=4 * MIB),
+        cost_estimate=pl.CostEstimate(
+            flops=0, bytes_accessed=2 * cent_dev * width + 4 * resid_words.size, transcendentals=0
+        ),
+        name="tables",
+    )(centroids, resid_words)
+
+
 def score_kernel(
     sizes,
     me_ref,
     cand_ref,
     own_ref,
     levels_ref,
-    cent_hbm,
-    words_hbm,
+    table,
+    staged,
+    words,
     codes_hbm,
     lens_hbm,
     *rest,
@@ -58,8 +112,8 @@
     group_count, cent_count, per_device, query_len, capacity, pass_dev, cand_count = sizes
     query_hbm = rest[:group_count]
     (
-        out_ref, staged, table, words, query_rows, query_t, own_t, dense, embed, maxima, ids_vmem, ids, codes, lens,
-        work, work_quad, item_pass, item_len, item_lane, table_sem, words_sem, query_sem, small_sem,
+        out_ref, query_rows, query_t, own_t, dense, embed, maxima, ids_vmem, ids, codes, lens,
+        work, work_quad, item_pass, item_len, item_lane, query_sem, small_sem,
     ) = rest[group_count:]
     sources = cand_ref.shape[0]
     pairs = per_device * cand_count
@@ -71,22 +125,6 @@
     group_quads = cent_count // quad_sources
     per_bits = per_device.bit_length() - 1
     tile_bits = tiles.bit_length() - 1
-    part_rows = staged.shape[0] // quads
-    word_parts = words_sem.shape[0]
-    part_pass = pass_dev // word_parts
-
-    def table_copy(part):
-        rows = pl.ds(pl.multiple_of(part * part_rows, part_rows), part_rows)
-        return pltpu.make_async_copy(cent_hbm.at[rows, :], staged.at[rows, :], table_sem.at[part])
-
-    def words_copy(part):
-        rows = pl.ds(part * part_pass, part_pass)
-        return pltpu.make_async_copy(words_hbm.at[rows], words.at[rows], words_sem.at[part])
-
-    def start_table(part, carry):
-        table_copy(part).start()
-        return carry
-
     group = jnp.bitwise_and(me_ref[0], group_count - 1)
 
     def query_copy(apart):
@@ -99,10 +137,7 @@
     lens_copy.start()
     for apart in range(group_count):
         query_copy(apart).start()
-    lax.fori_loop(0, quads, start_table, 0)
     codes_copy.start()
-    for part in range(word_parts):
-        words_copy(part).start()
 
     first = me_ref[0] * pass_dev
     local = cand_ref[...] - first
@@ -137,9 +172,6 @@
     spare = items * tiles
 
     def prepare(quad, count):
-        table_copy(quad).wait()
-        rows = pl.ds(pl.multiple_of(quad * part_rows, part_rows), part_rows)
-        table[rows, :] = staged[rows, :].astype(jnp.float32)
         block = query_rows[quad // group_quads, pl.ds(quad % group_quads * LANES, LANES), :]
         query_t[quad] = jnp.transpose(block.astype(jnp.float32)).astype(jnp.bfloat16)
         start = count
@@ -173,8 +205,6 @@
         work_quad[total // ALIGN + index] = 0
     chunks = jnp.maximum((total + BLOCKS - 1) // BLOCKS, 2)
     codes_copy.wait()
-    for part in range(word_parts):
-        words_copy(part).wait()
 
     sub = lax.broadcasted_iota(jnp.int32, (SUB, LANES), 0)
     position = jnp.concatenate([sub * FIELDS + field for field in range(FIELDS)], axis=0)
@@ -274,7 +304,9 @@
         out_ref[source, :, best_lanes:] = by_source[source : source + 1, :]
 
 
-def owner_scores(me, cand_all, query_parts, centroids, token_codes, resid_words, lengths, levels, sizes):
+def owner_scores(me, cand_all, query_parts, held, token_codes, lengths, levels, sizes):
+    held = [pltpu.with_memory_space_constraint(array, pltpu.VMEM) for array in held]
+    _, centroids, resid_words = held
     capacity = sizes[4]
     sources = cand_all.shape[0]
     group_count = len(query_parts)
@@ -291,13 +323,10 @@
     tokens = items * plen
     return pl.pallas_call(
         functools.partial(score_kernel, sizes),
-        in_specs=[pl.BlockSpec(memory_space=pltpu.SMEM), vmem, vmem, vmem] + [any_space] * (4 + group_count),
+        in_specs=[pl.BlockSpec(memory_space=pltpu.SMEM), vmem, vmem, vmem, vmem, vmem, vmem] + [any_space] * (2 + group_count),
         out_specs=vmem,
         out_shape=jax.ShapeDtypeStruct((sources, 1, group_rows + LANES), jnp.float32),
         scratch_shapes=[
-            pltpu.VMEM((cent_dev, width), jnp.bfloat16),
-            pltpu.VMEM((cent_dev + SUB, width), jnp.float32),
-            pltpu.VMEM((pass_dev, packed, width), jnp.int32),
             pltpu.VMEM((group_count, group_rows, width), jnp.bfloat16),
             pltpu.VMEM((quads, width, LANES), jnp.bfloat16),
             pltpu.VMEM((width, group_rows), jnp.bfloat16),
@@ -313,18 +342,16 @@
             pltpu.SMEM((items + 1,), jnp.int32),
             pltpu.SMEM((items + 1,), jnp.int32),
             pltpu.SMEM((items + 1,), jnp.int32),
-            pltpu.SemaphoreType.DMA((quads,)),
-            pltpu.SemaphoreType.DMA((4,)),
             pltpu.SemaphoreType.DMA((group_count,)),
             pltpu.SemaphoreType.DMA((3,)),
         ],
-        compiler_params=pltpu.CompilerParams(vmem_limit_bytes=56 * MIB),
+        compiler_params=pltpu.CompilerParams(vmem_limit_bytes=16 * MIB),
         cost_estimate=pl.CostEstimate(
             flops=2 * (tokens * LANES + cent_dev * group_rows) * width, bytes_accessed=2 * cent_dev * width * 2, transcendentals=tokens
         ),
         name="owner_scores",
     )(
-        me, cand_all, query_parts[0], levels, centroids, resid_words, token_codes.reshape(pass_dev * plen), lengths, *query_parts
+        me, cand_all, query_parts[0], levels, *held, token_codes.reshape(pass_dev * plen), lengths, *query_parts
     )
 
 
@@ -392,7 +419,7 @@
         pairs = [(index, index ^ apart) for index in range(group_count)]
         query_parts.append(lax.ppermute(query_rows, "grp", pairs))
     reply = owner_scores(
-        me, cand_all, query_parts, centroids, token_codes, resid_words, lengths, levels, sizes
+        me, cand_all, query_parts, tables(centroids, resid_words), token_codes, lengths, levels, sizes
     )
     back = lax.all_to_all(reply, ("cent", "grp"), split_axis=0, concat_axis=0, tiled=True)
     token_best, scores = finish(me, back, cand, group_rows, sizes)

time: 68.4 us -> 92.5 us (1.35)
  local copies, waits for them, and re-layouts: 0.7 us -> 24.7 us
  blocking collectives: 11.1 us -> 23.1 us
  waiting for transfers between devices: 7.15 us -> 0.01 us
  Pallas kernels: 39.2 us -> 35 us
    unnamed x8 -> x20, local copies, waits for them, and re-layouts: 0.7 us -> 24.7 us
    all_to_all x1, blocking collectives: 11.1 us -> 23.1 us  [shards(): lax.all_to_all(reply, ('cent', 'grp'), split_axis=0, concat_axis=0, tiled...]
    pallas_call x1, Pallas kernels: 35.9 us -> 25.6 us  [owner_scores(): pl.pallas_call(functools.partial(score_kernel, sizes), in_specs=[pl.Block...]
    all_to_all x1, waiting for transfers between devices: 7.14 us -> 0.01 us  [shards(): lax.all_to_all(ids_for_all(cand, devices), ('cent', 'grp'), split_axis=0,...]
    pallas_call x0 -> x1, Pallas kernels: none -> 6.1 us  [tables(): pl.pallas_call(tables_kernel, in_specs=[pl.BlockSpec(memory_space=pltpu.H...]
  transfers between devices with their start and end apart: 4 -> 4, of which waited for: 1 -> 0; matrix products, arithmetic and copies ran while one was open for 0% -> 0% of each run, Pallas kernels for 2% -> 8%
where the time goes in v1:
time: 92.5 us; the launch traced here: 92.9 us
  Pallas kernels  35 us (38%)
  local copies, waits for them, and re-layouts  24.7 us (27%)
  blocking collectives  23.1 us (25%)
  starting transfers between devices  9.22 us (10%)
    pallas_call x1, Pallas kernels, owner_scores(): pl.pallas_call(functools.partial(score_kernel, sizes), in_specs=[pl.Block...  25.6 us
    unnamed x20, local copies, waits for them, and re-layouts  24.7 us
    all_to_all x1, blocking collectives, shards(): lax.all_to_all(reply, ('cent', 'grp'), split_axis=0, concat_axis=0, tiled...  23.1 us
    pallas_call x1, Pallas kernels, tables(): pl.pallas_call(tables_kernel, in_specs=[pl.BlockSpec(memory_space=pltpu.H...  6.1 us
    all_to_all x1, starting transfers between devices, shards(): lax.all_to_all(ids_for_all(cand, devices), ('cent', 'grp'), split_axis=0,...  6.1 us
    ppermute x3, starting transfers between devices, shards(): query_parts.append(lax.ppermute(query_rows, 'grp', pairs))  3.12 us
    pallas_call x1, Pallas kernels, finish(): pl.pallas_call(functools.partial(finish_kernel, sizes), in_specs=[pl.Bloc...  1.97 us
  transfers between devices with their start and end apart: 4, of which 0 were waited for; matrix products, arithmetic and copies ran while one was open for 0% of the time, Pallas kernels for 8%

profile of v1, /device:TPU:0, one launch (start us, length us, event | category | flops | bytes accessed | tf_op | source)
XLA Modules:
  0.0 92.9 jit_solution(7310415836332695861)
XLA Ops:
  0.6 2.4 %collective-permute-start.2 = (bf16[512,128]{1,0:T(8,128)(2,1)}, bf16[512,128]{1,0:T(8,128)(2,1)S(1)}, u32[]{:S(2)}, u32[]{:S(2)}) collective-permute-start(bf16[512,128]{1,0:T(8,128)(2,1)} %bitcast.9), channel_id=1, source_target_pairs={{0,3},{1,2},{2,1},{3,0},{4,7},{5,6},{6,5},{7,4},{8,11},{9,10},{10,... | collective-permute-start | bytes 393224 | tf_op jit(solution)/shard_map/ppermute | solution.py:420
  3.1 0.6 collective-permute-start.1
  3.7 0.0 collective-permute-start
  3.8 1.3 %ids_for_all.1 = s32[32,128]{1,0:T(8,128)} custom-call(s32[2,64]{1,0:T(2,128)} %bitcast.17), custom_call_target="tpu_custom_call" | custom-call | tf_op jit(solution)/shard_map/ids_for_all/pallas_call | solution.py:39
  5.1 6.1 %all-to-all-start = ((s32[32,1,128]{2,1,0:T(1,128)}), s32[32,1,128]{2,1,0:T(1,128)S(1)}, u32[]{:S(2)}, u32[]{:S(2)}) async-start(s32[32,1,128]{2,1,0:T(1,128)} %bitcast.16), calls=%async_computation | async-start | bytes 32768 | tf_op jit(solution)/shard_map/all_to_all | solution.py:414
  11.2 0.0 copy-start.6
  11.2 0.0 copy-start.7
  11.2 0.0 copy-start.8
  11.3 0.0 copy-start.9
  11.3 6.1 %tables.1 = (f32[32776,128]{1,0:T(8,128)S(1)}, bf16[32768,128]{1,0:T(8,128)(2,1)S(1)}, s32[512,32,128]{2,1,0:T(8,128)S(1)}) custom-call(bf16[32768,128]{1,0:T(8,128)(2,1)} %cent_hbm.1, s32[512,32,128]{2,1,0:T(8,128)} %words_hbm.1), custom_call_target="tpu_custom_call" | custom-call | bytes 16777216 | tf_op jit(solution)/shard_map/tables/pallas_call | solution.py:81
  17.4 0.0 copy-start
  17.4 5.7 %copy-done = f32[32776,128]{1,0:T(8,128)} copy-done((f32[32776,128]{1,0:T(8,128)}, f32[32776,128]{1,0:T(8,128)S(1)}, u32[]{:S(2)}) %copy-start) | copy-done | bytes 16781336
  23.1 0.0 copy-start.2
  23.1 3.2 %copy-done.2 = bf16[32768,128]{1,0:T(8,128)(2,1)} copy-done((bf16[32768,128]{1,0:T(8,128)(2,1)}, bf16[32768,128]{1,0:T(8,128)(2,1)S(1)}, u32[]{:S(2)}) %copy-start.2) | copy-done | bytes 8388632
  26.3 0.0 copy-start.4
  26.4 3.2 %copy-done.4 = s32[512,32,128]{2,1,0:T(8,128)} copy-done((s32[512,32,128]{2,1,0:T(8,128)}, s32[512,32,128]{2,1,0:T(8,128)S(1)}, u32[]{:S(2)}) %copy-start.4) | copy-done | bytes 8388632
  29.6 0.0 all-to-all-done
  29.6 0.0 collective-permute-done.2.rest_3_
  29.6 0.0 collective-permute-done.1.rest_2_
  29.6 0.0 collective-permute-done.rest_1_
  29.6 0.0 copy-done.6
  29.6 0.0 copy-done.7
  29.6 0.0 copy-done.8
  29.6 0.0 copy-done.9
  29.6 0.0 copy-start.1
  29.7 5.8 %copy-done.1 = f32[32776,128]{1,0:T(8,128)S(1)} copy-done((f32[32776,128]{1,0:T(8,128)S(1)}, f32[32776,128]{1,0:T(8,128)}, u32[]{:S(2)}) %copy-start.1) | copy-done | bytes 16781336
  35.4 0.0 copy-start.3
  35.4 3.4 %copy-done.3 = bf16[32768,128]{1,0:T(8,128)(2,1)S(1)} copy-done((bf16[32768,128]{1,0:T(8,128)(2,1)S(1)}, bf16[32768,128]{1,0:T(8,128)(2,1)}, u32[]{:S(2)}) %copy-start.3) | copy-done | bytes 8388632
  38.8 3.4 %copy-done.5 = s32[512,32,128]{2,1,0:T(8,128)S(1)} copy-done((s32[512,32,128]{2,1,0:T(8,128)S(1)}, s32[512,32,128]{2,1,0:T(8,128)}, u32[]{:S(2)}) %copy-start.5) | copy-done | bytes 8388632
  42.2 25.6 %owner_scores.1 = f32[32,1,640]{2,1,0:T(1,128)S(1)} custom-call(s32[1]{0:T(128)} %bitcast.me_ref, s32[32,128]{1,0:T(8,128)S(1)} %bitcast.15, bf16[512,128]{1,0:T(8,128)(2,1)S(1)} %bitcast.12, f32[4,128]{1,0:T(4,128)S(1)} %copy-done.8, f32[32776,128]{1,0:T(8,128)S(1)} %copy-done.1, bf16[32768,128]{1,0:T(8,128)(2,1)S(1)} %copy-done.3, ...), custom_call_target="tpu_custom_call" | custom-call | flops 5368709120 | bytes 16777216 | tf_op jit(solution)/shard_map/owner_scores/pallas_call | solution.py:324
  67.8 23.1 %all_to_all.16.back_ref = f32[32,1,640]{2,1,0:T(1,128)} all-to-all(f32[32,1,640]{2,1,0:T(1,128)S(1)} %owner_scores.1), channel_id=1, replica_groups=mesh['cent'=8,'grp'=4] {'cent','grp'}, dimensions={0} | all-to-all | bytes 163840 | tf_op jit(solution)/shard_map/all_to_all | solution.py:424
  90.9 2.0 %finish.1 = (f32[16,32]{1,0:T(8,128)}, f32[2,64]{1,0:T(2,128)}) custom-call(s32[1]{0:T(128)} %bitcast.me_ref, f32[32,1,640]{2,1,0:T(1,128)} %all_to_all.16.back_ref, s32[2,64]{1,0:T(2,128)} %bitcast.18), custom_call_target="tpu_custom_call" | custom-call | tf_op jit(solution)/shard_map/finish/pallas_call | solution.py:389
  (1 shorter events, 0.0 us)
Async XLA Ops:
  0.6 29.0 %collective-permute-start.2 = (bf16[512,128]{1,0:T(8,128)(2,1)}, bf16[512,128]{1,0:T(8,128)(2,1)S(1)}, u32[]{:S(2)}, u32[]{:S(2)}) collective-permute-start(bf16[512,128]{1,0:T(8,128)(2,1)} %bitcast.9), channel_id=1, source_target_pairs={{0,3},{1,2},{2,1},{3,0},{4,7},{5,6},{6,5},{7,4},{8,11},{9,10},{10,... | collective-permute-start | bytes 393224 | tf_op jit(solution)/shard_map/ppermute | solution.py:420
  3.1 26.5 %collective-permute-start.1 = (bf16[512,128]{1,0:T(8,128)(2,1)}, bf16[512,128]{1,0:T(8,128)(2,1)S(1)}, u32[]{:S(2)}, u32[]{:S(2)}) collective-permute-start(bf16[512,128]{1,0:T(8,128)(2,1)} %bitcast.10), channel_id=1, source_target_pairs={{0,2},{1,3},{2,0},{3,1},{4,6},{5,7},{6,4},{7,5},{8,10},{9,11},{10,... | collective-permute-start | bytes 393224 | tf_op jit(solution)/shard_map/ppermute | solution.py:420
  3.7 25.9 %collective-permute-start = (bf16[512,128]{1,0:T(8,128)(2,1)}, bf16[512,128]{1,0:T(8,128)(2,1)S(1)}, u32[]{:S(2)}, u32[]{:S(2)}) collective-permute-start(bf16[512,128]{1,0:T(8,128)(2,1)} %bitcast.11), channel_id=1, source_target_pairs={{0,1},{1,0},{2,3},{3,2},{4,5},{5,4},{6,7},{7,6},{8,9},{9,8},{10,11... | collective-permute-start | bytes 393224 | tf_op jit(solution)/shard_map/ppermute | solution.py:420
  5.1 24.5 %all-to-all-start = ((s32[32,1,128]{2,1,0:T(1,128)}), s32[32,1,128]{2,1,0:T(1,128)S(1)}, u32[]{:S(2)}, u32[]{:S(2)}) async-start(s32[32,1,128]{2,1,0:T(1,128)} %bitcast.16), calls=%async_computation | async-start | bytes 32768 | tf_op jit(solution)/shard_map/all_to_all | solution.py:414
  11.2 18.4 %copy-start.6 = (bf16[16,32,128]{2,1,0:T(8,128)(2,1)S(1)}, bf16[16,32,128]{2,1,0:T(8,128)(2,1)}, u32[]{:S(2)}) copy-start(bf16[16,32,128]{2,1,0:T(8,128)(2,1)} %param.7) | copy-start | bytes 393220
  11.2 18.4 %copy-start.7 = (s32[512,128]{1,0:T(8,128)S(1)}, s32[512,128]{1,0:T(8,128)}, u32[]{:S(2)}) copy-start(s32[512,128]{1,0:T(8,128)} %param.10) | copy-start | bytes 786436
  11.2 18.4 %copy-start.8 = (f32[4,128]{1,0:T(4,128)S(1)}, f32[4,128]{1,0:T(4,128)}, u32[]{:S(2)}) copy-start(f32[4,128]{1,0:T(4,128)} %levels_ref.1) | copy-start | bytes 6148
  11.3 18.4 %copy-start.9 = (s32[512]{0:T(512)S(1)}, s32[512]{0:T(512)}, u32[]{:S(2)}) copy-start(s32[512]{0:T(512)} %lens_hbm.1) | copy-start | bytes 6148
  17.4 5.7 %copy-start = (f32[32776,128]{1,0:T(8,128)}, f32[32776,128]{1,0:T(8,128)S(1)}, u32[]{:S(2)}) copy-start(f32[32776,128]{1,0:T(8,128)S(1)} %get-tuple-element.7.table) | copy-start | bytes 50343940
  23.1 3.2 %copy-start.2 = (bf16[32768,128]{1,0:T(8,128)(2,1)}, bf16[32768,128]{1,0:T(8,128)(2,1)S(1)}, u32[]{:S(2)}) copy-start(bf16[32768,128]{1,0:T(8,128)(2,1)S(1)} %get-tuple-element.8.staged) | copy-start | bytes 25165828
  26.3 3.2 %copy-start.4 = (s32[512,32,128]{2,1,0:T(8,128)}, s32[512,32,128]{2,1,0:T(8,128)S(1)}, u32[]{:S(2)}) copy-start(s32[512,32,128]{2,1,0:T(8,128)S(1)} %get-tuple-element.9.words) | copy-start | bytes 25165828
  29.6 5.8 %copy-start.1 = (f32[32776,128]{1,0:T(8,128)S(1)}, f32[32776,128]{1,0:T(8,128)}, u32[]{:S(2)}) copy-start(f32[32776,128]{1,0:T(8,128)} %copy-done) | copy-start | bytes 50343940
  35.4 3.4 %copy-start.3 = (bf16[32768,128]{1,0:T(8,128)(2,1)S(1)}, bf16[32768,128]{1,0:T(8,128)(2,1)}, u32[]{:S(2)}) copy-start(bf16[32768,128]{1,0:T(8,128)(2,1)} %copy-done.2) | copy-start | bytes 25165828
  38.8 3.4 %copy-start.5 = (s32[512,32,128]{2,1,0:T(8,128)S(1)}, s32[512,32,128]{2,1,0:T(8,128)}, u32[]{:S(2)}) copy-start(s32[512,32,128]{2,1,0:T(8,128)} %copy-done.4) | copy-start | bytes 25165828

commit v2 on v0

--- a/solution.py
+++ b/solution.py
@@ -58,9 +58,10 @@
     group_count, cent_count, per_device, query_len, capacity, pass_dev, cand_count = sizes
     query_hbm = rest[:group_count]
     (
-        out_ref, staged, table, words, query_rows, query_t, own_t, dense, embed, maxima, ids_vmem, ids, codes, lens,
-        work, work_quad, item_pass, item_len, item_lane, table_sem, words_sem, query_sem, small_sem,
+        out_ref, staged, table, words, query_rows, query_t, own_t, dense, embed, maxima, ids_vmem, ids, codes,
+        word_stage, code_stage, slot_even, slot_odd, lens, work, work_quad, item_pass, item_len, item_lane, table_sem, words_sem, query_sem, small_sem, slot_sem,
     ) = rest[group_count:]
+    code_slots = (slot_even, slot_odd)
     sources = cand_ref.shape[0]
     pairs = per_device * cand_count
     items = sources * capacity
@@ -143,22 +144,21 @@
         block = query_rows[quad // group_quads, pl.ds(quad % group_quads * LANES, LANES), :]
         query_t[quad] = jnp.transpose(block.astype(jnp.float32)).astype(jnp.bfloat16)
         start = count
+        found = []
         for part in range(quad_sources):
             cent = quad % group_quads * quad_sources + part
             source = cent * group_count + quad // group_quads
-            for slot in range(capacity):
-                tag = ids[source, slot] - 1
-                item = source * capacity + slot
-                real = tag >= 0
-                held = jnp.maximum(tag, 0)
-                passage = jnp.right_shift(held, per_bits)
-                length = lens[passage]
-                item_pass[item] = passage
-                item_len[item] = length
-                item_lane[item] = part * per_device + jnp.bitwise_and(held, per_device - 1)
-                for tile in range(tiles):
-                    work[count + tile] = item * tiles + tile
-                count = count + jnp.where(real, jnp.right_shift(length + tile_tokens - 1, tile_tokens.bit_length() - 1), 0)
+            found += [(part, source * capacity + slot, ids[source, slot] - 1) for slot in range(capacity)]
+        found = [(part, item, tag, jnp.maximum(tag, 0)) for part, item, tag in found]
+        lengths = [lens[jnp.right_shift(held, per_bits)] for _, _, _, held in found]
+        for (part, item, tag, held), length in zip(found, lengths):
+            item_pass[item] = jnp.right_shift(held, per_bits)
+            item_len[item] = length
+            item_lane[item] = part * per_device + jnp.bitwise_and(held, per_device - 1)
+            for tile in range(tiles):
+                work[count + tile] = item * tiles + tile
+            blocks = jnp.right_shift(length + tile_tokens - 1, tile_tokens.bit_length() - 1)
+            count = count + jnp.where(tag >= 0, blocks, 0)
         for index in range(ALIGN):
             work[count + index] = spare
         count = (count + ALIGN - 1) // ALIGN * ALIGN
@@ -167,17 +167,19 @@
         return count
 
     total = lax.fori_loop(0, quads, prepare, 0)
-    for index in range(2 * BLOCKS):
+    for index in range(4 * BLOCKS):
         work[total + index] = spare
-    for index in range(2 * BLOCKS // ALIGN):
+    for index in range(4 * BLOCKS // ALIGN):
         work_quad[total // ALIGN + index] = 0
-    chunks = jnp.maximum((total + BLOCKS - 1) // BLOCKS, 2)
+    pairs_of_chunks = jnp.maximum((total + 2 * BLOCKS - 1) // (2 * BLOCKS), 1)
     codes_copy.wait()
     for part in range(word_parts):
         words_copy(part).wait()
 
     sub = lax.broadcasted_iota(jnp.int32, (SUB, LANES), 0)
     position = jnp.concatenate([sub * FIELDS + field for field in range(FIELDS)], axis=0)
+    row_blocks = LANES // tile_tokens
+    lane_tile = lax.broadcasted_iota(jnp.int32, (1, LANES), 1) // tile_tokens
     lane_group = lax.broadcasted_iota(jnp.int32, (1, LANES), 1) // query_len
     level = [levels_ref[index : index + 1, :] for index in range(FIELDS)]
 
@@ -196,17 +198,33 @@
             best = jnp.max(kept, axis=0, keepdims=True)
             maxima[tile, pl.ds(item, 1), :] = jnp.where(lane_group == item_lane[item], best, 0.0)
 
-    def decode(chunk):
+    def slot_copy(slot):
+        return pltpu.make_async_copy(code_stage.at[slot], code_slots[slot], slot_sem.at[slot])
+
+    def fetch(chunk, slot):
+        for row in range(BLOCKS // row_blocks):
+            together = jnp.zeros((1, LANES), jnp.int32)
+            for index in range(row_blocks):
+                block = row * row_blocks + index
+                entry = work[chunk * BLOCKS + block]
+                passage = item_pass[jnp.right_shift(entry, tile_bits)]
+                tile = jnp.bitwise_and(entry, tiles - 1)
+                shift = jnp.bitwise_and(index - tile, row_blocks - 1) * tile_tokens
+                moved = pltpu.roll(codes[pl.ds(passage, 1), :], shift, 1)
+                together = jnp.where(lane_tile == index, moved, together)
+                rows = pl.ds(pl.multiple_of(tile * SUB, SUB), SUB)
+                word_stage[slot, block * SUB : (block + 1) * SUB, :] = words[passage, rows, :]
+            code_stage[slot, row : row + 1, :] = together
+        slot_copy(slot).start()
+
+    def decode(slot):
         for index in range(BLOCKS):
-            entry = work[chunk * BLOCKS + index]
-            item, tile = jnp.right_shift(entry, tile_bits), jnp.bitwise_and(entry, tiles - 1)
-            passage = item_pass[item]
-            start = passage * (tiles * tile_tokens) + tile * tile_tokens
-            word = words[passage, pl.ds(pl.multiple_of(tile * SUB, SUB), SUB), :]
+            word = word_stage[slot, index * SUB : (index + 1) * SUB, :]
             for field in range(FIELDS):
                 rows = jnp.zeros((SUB, LANES), jnp.float32)
                 for row in range(SUB):
-                    code = codes[start + (row * FIELDS + field)]
+                    place = index % row_blocks * tile_tokens + row * FIELDS + field
+                    code = code_slots[slot][index // row_blocks, place]
                     rows = jnp.where(sub == row, table[pl.ds(code, SUB, stride=0), :], rows)
                 low = jnp.bitwise_and(word, 1 << (2 * field)) != 0
                 high = jnp.bitwise_and(word, 2 << (2 * field)) != 0
@@ -231,28 +249,47 @@
         scores = jnp.dot(block, own_t[...], preferred_element_type=jnp.float32)
         return jnp.maximum(best, jnp.max(scores.reshape(tile_rows // SUB, SUB, scores.shape[1]), axis=0))
 
+    fetch(0, 0)
+    fetch(1, 1)
+    slot_copy(0).wait()
     decode(0)
+    fetch(2, 0)
     normalize()
+    slot_copy(1).wait()
     decode(1)
-
-    def step(chunk, carry):
-        score(chunk - 2)
-        normalize()
-        decode(chunk)
+    fetch(3, 1)
+
+    def step(pair, carry):
+        for slot in range(2):
+            chunk = 2 * pair + slot
+            slot_copy(slot).wait()
+            score(chunk - 2)
+            normalize()
+            decode(slot)
+            fetch(chunk + 2, slot)
         return carry
 
-    def step_with_tile(chunk, best):
-        step(chunk, 0)
-        return centroid_tile(chunk - 2, best)
+    def step_with_tile(pair, best):
+        for slot in range(2):
+            chunk = 2 * pair + slot
+            slot_copy(slot).wait()
+            score(chunk - 2)
+            normalize()
+            decode(slot)
+            best = centroid_tile(chunk - 2, best)
+            fetch(chunk + 2, slot)
+        return best
 
     token_best = jnp.full((SUB, own_t.shape[1]), -jnp.inf, jnp.float32)
-    shared = jnp.minimum(chunks, best_tiles + 2)
-    token_best = lax.fori_loop(2, shared, step_with_tile, token_best)
-    lax.fori_loop(shared, chunks, step, 0)
-    score(chunks - 2)
+    shared = jnp.minimum(pairs_of_chunks, best_tiles // 2 + 1)
+    token_best = lax.fori_loop(1, shared, step_with_tile, token_best)
+    lax.fori_loop(shared, pairs_of_chunks, step, 0)
+    score(2 * pairs_of_chunks - 2)
     normalize()
-    score(chunks - 1)
-    token_best = lax.fori_loop(shared - 2, best_tiles, centroid_tile, token_best)
+    score(2 * pairs_of_chunks - 1)
+    for slot in range(2):
+        slot_copy(slot).wait()
+    token_best = lax.fori_loop(2 * (shared - 1), best_tiles, centroid_tile, token_best)
     token_best = jnp.max(token_best, axis=0, keepdims=True)
 
     best = maxima[0, :items, :]
@@ -285,7 +322,7 @@
     tiles = packed // SUB
     items = sources * capacity
     quads = group_count * group_rows // LANES
-    work_size = items * tiles + quads * ALIGN + 2 * BLOCKS
+    work_size = items * tiles + quads * ALIGN + 4 * BLOCKS
     any_space = pl.BlockSpec(memory_space=pl.ANY)
     vmem = pl.BlockSpec(memory_space=pltpu.VMEM)
     tokens = items * plen
@@ -306,7 +343,11 @@
             pltpu.VMEM((tiles, items + SUB, LANES), jnp.float32),
             pltpu.VMEM((sources, LANES), jnp.int32),
             pltpu.SMEM((sources, LANES), jnp.int32),
-            pltpu.SMEM((pass_dev * plen,), jnp.int32),
+            pltpu.VMEM((pass_dev, plen), jnp.int32),
+            pltpu.VMEM((2, BLOCKS * SUB, LANES), jnp.int32),
+            pltpu.VMEM((2, BLOCKS * SUB * FIELDS // LANES, LANES), jnp.int32),
+            pltpu.SMEM((BLOCKS * SUB * FIELDS // LANES, LANES), jnp.int32),
+            pltpu.SMEM((BLOCKS * SUB * FIELDS // LANES, LANES), jnp.int32),
             pltpu.SMEM((pass_dev,), jnp.int32),
             pltpu.SMEM((work_size,), jnp.int32),
             pltpu.SMEM((work_size // ALIGN + items * tiles // quads,), jnp.int32),
@@ -317,6 +358,7 @@
             pltpu.SemaphoreType.DMA((4,)),
             pltpu.SemaphoreType.DMA((group_count,)),
             pltpu.SemaphoreType.DMA((3,)),
+            pltpu.SemaphoreType.DMA((2,)),
         ],
         compiler_params=pltpu.CompilerParams(vmem_limit_bytes=56 * MIB),
         cost_estimate=pl.CostEstimate(
@@ -324,7 +366,7 @@
         ),
         name="owner_scores",
     )(
-        me, cand_all, query_parts[0], levels, centroids, resid_words, token_codes.reshape(pass_dev * plen), lengths, *query_parts
+        me, cand_all, query_parts[0], levels, centroids, resid_words, token_codes, lengths, *query_parts
     )
 
 

time: 68.4 us -> 66.3 us (0.969); the launches traced: 68.1 us -> 67.3 us
  Pallas kernels: 39.2 us -> 29.6 us
  blocking collectives: 11.1 us -> 20 us
    pallas_call x1, Pallas kernels: 35.9 us -> 26.2 us  [owner_scores(): pl.pallas_call(functools.partial(score_kernel, sizes), in_specs=[pl.Block...]
    all_to_all x1, blocking collectives: 11.1 us -> 20 us  [shards(): lax.all_to_all(reply, ('cent', 'grp'), split_axis=0, concat_axis=0, tiled...]
where the time goes in v2:
time: 66.3 us; the launch traced here: 67.3 us
  Pallas kernels  29.6 us (45%)
  blocking collectives  20 us (30%)
  starting transfers between devices  9.22 us (14%)
  waiting for transfers between devices  7.15 us (11%)
  local copies, waits for them, and re-layouts  0.7 us (1%)
  between operations  0.69 us (1%)
    pallas_call x1, Pallas kernels, owner_scores(): pl.pallas_call(functools.partial(score_kernel, sizes), in_specs=[pl.Block...  26.2 us
    all_to_all x1, blocking collectives, shards(): lax.all_to_all(reply, ('cent', 'grp'), split_axis=0, concat_axis=0, tiled...  20 us
    all_to_all x1, waiting for transfers between devices, shards(): lax.all_to_all(ids_for_all(cand, devices), ('cent', 'grp'), split_axis=0,...  7.14 us
    all_to_all x1, starting transfers between devices, shards(): lax.all_to_all(ids_for_all(cand, devices), ('cent', 'grp'), split_axis=0,...  6.1 us
    ppermute x3, starting transfers between devices, shards(): query_parts.append(lax.ppermute(query_rows, 'grp', pairs))  3.12 us
    pallas_call x1, Pallas kernels, finish(): pl.pallas_call(functools.partial(finish_kernel, sizes), in_specs=[pl.Bloc...  1.97 us
    pallas_call x1, Pallas kernels, ids_for_all(): pl.pallas_call(ids_kernel, in_specs=[vmem], out_specs=vmem, out_shape=jax...  1.35 us
  transfers between devices with their start and end apart: 4, of which 1 were waited for; matrix products, arithmetic and copies ran while one was open for 0% of the time, Pallas kernels for 2%

profile of v2, /device:TPU:0, one launch (start us, length us, event | category | flops | bytes accessed | tf_op | source)
XLA Modules:
  0.0 67.3 jit_solution(9667620060091060921)
XLA Ops:
  0.6 2.4 %collective-permute-start.2 = (bf16[512,128]{1,0:T(8,128)(2,1)}, bf16[512,128]{1,0:T(8,128)(2,1)S(1)}, u32[]{:S(2)}, u32[]{:S(2)}) collective-permute-start(bf16[512,128]{1,0:T(8,128)(2,1)} %bitcast.12), channel_id=1, source_target_pairs={{0,3},{1,2},{2,1},{3,0},{4,7},{5,6},{6,5},{7,4},{8,11},{9,10},{10,... | collective-permute-start | bytes 393224 | tf_op jit(solution)/shard_map/ppermute | solution.py:435
  3.1 0.6 collective-permute-start.1
  3.7 0.0 collective-permute-start
  3.8 1.3 %ids_for_all.1 = s32[32,128]{1,0:T(8,128)} custom-call(s32[2,64]{1,0:T(2,128)} %bitcast.10), custom_call_target="tpu_custom_call" | custom-call | tf_op jit(solution)/shard_map/ids_for_all/pallas_call | solution.py:37
  5.1 6.1 %all-to-all-start = ((s32[32,1,128]{2,1,0:T(1,128)}), s32[32,1,128]{2,1,0:T(1,128)S(1)}, u32[]{:S(2)}, u32[]{:S(2)}) async-start(s32[32,1,128]{2,1,0:T(1,128)} %bitcast.8), calls=%async_computation | async-start | bytes 32768 | tf_op jit(solution)/shard_map/all_to_all | solution.py:429
  11.2 7.1 %all-to-all-done = s32[32,1,128]{2,1,0:T(1,128)S(1)} async-done(((s32[32,1,128]{2,1,0:T(1,128)}), s32[32,1,128]{2,1,0:T(1,128)S(1)}, u32[]{:S(2)}, u32[]{:S(2)}) %all-to-all-start) | async-done | bytes 16416 | tf_op jit(solution)/shard_map/all_to_all | solution.py:429
  18.4 0.0 copy-start
  18.4 0.0 collective-permute-done.2.rest_3_
  18.4 0.0 copy-start.1
  18.4 0.0 collective-permute-done.1.rest_2_
  18.4 0.0 copy-start.2
  18.4 0.0 collective-permute-done.rest_1_
  18.4 0.0 copy-start.3
  18.4 0.6 copy-done
  18.9 0.1 copy-done.1
  19.0 0.1 copy-done.2
  19.1 0.0 copy-done.3
  19.1 26.2 %owner_scores.1 = f32[32,1,640]{2,1,0:T(1,128)} custom-call(s32[1]{0:T(128)} %bitcast.me_ref, s32[32,128]{1,0:T(8,128)} %bitcast.9, bf16[512,128]{1,0:T(8,128)(2,1)} %bitcast.15, f32[4,128]{1,0:T(4,128)} %levels_ref.1, bf16[32768,128]{1,0:T(8,128)(2,1)} %cent_hbm.1, s32[512,32,128]{2,1,0:T(8,128)} %words_hbm.1, s32[512,128]{1,0:T(8,128)} %codes_hbm.1, ...), custom_call_target="tpu_custom_call" | custom-call | flops 5368709120 | bytes 16777216 | tf_op jit(solution)/shard_map/owner_scores/pallas_call | solution.py:329
  45.3 20.0 %all_to_all.16.back_ref = f32[32,1,640]{2,1,0:T(1,128)} all-to-all(f32[32,1,640]{2,1,0:T(1,128)} %owner_scores.1), channel_id=1, replica_groups=mesh['cent'=8,'grp'=4] {'cent','grp'}, dimensions={0} | all-to-all | bytes 163840 | tf_op jit(solution)/shard_map/all_to_all | solution.py:439
  65.3 2.0 %finish.1 = (f32[16,32]{1,0:T(8,128)}, f32[2,64]{1,0:T(2,128)}) custom-call(s32[1]{0:T(128)} %bitcast.me_ref, f32[32,1,640]{2,1,0:T(1,128)} %all_to_all.16.back_ref, s32[2,64]{1,0:T(2,128)} %bitcast.11), custom_call_target="tpu_custom_call" | custom-call | tf_op jit(solution)/shard_map/finish/pallas_call | solution.py:404
Async XLA Ops:
  0.6 17.7 %collective-permute-start.2 = (bf16[512,128]{1,0:T(8,128)(2,1)}, bf16[512,128]{1,0:T(8,128)(2,1)S(1)}, u32[]{:S(2)}, u32[]{:S(2)}) collective-permute-start(bf16[512,128]{1,0:T(8,128)(2,1)} %bitcast.12), channel_id=1, source_target_pairs={{0,3},{1,2},{2,1},{3,0},{4,7},{5,6},{6,5},{7,4},{8,11},{9,10},{10,... | collective-permute-start | bytes 393224 | tf_op jit(solution)/shard_map/ppermute | solution.py:435
  3.1 15.3 %collective-permute-start.1 = (bf16[512,128]{1,0:T(8,128)(2,1)}, bf16[512,128]{1,0:T(8,128)(2,1)S(1)}, u32[]{:S(2)}, u32[]{:S(2)}) collective-permute-start(bf16[512,128]{1,0:T(8,128)(2,1)} %bitcast.13), channel_id=1, source_target_pairs={{0,2},{1,3},{2,0},{3,1},{4,6},{5,7},{6,4},{7,5},{8,10},{9,11},{10,... | collective-permute-start | bytes 393224 | tf_op jit(solution)/shard_map/ppermute | solution.py:435
  3.7 14.7 %collective-permute-start = (bf16[512,128]{1,0:T(8,128)(2,1)}, bf16[512,128]{1,0:T(8,128)(2,1)S(1)}, u32[]{:S(2)}, u32[]{:S(2)}) collective-permute-start(bf16[512,128]{1,0:T(8,128)(2,1)} %bitcast.14), channel_id=1, source_target_pairs={{0,1},{1,0},{2,3},{3,2},{4,5},{5,4},{6,7},{7,6},{8,9},{9,8},{10,11... | collective-permute-start | bytes 393224 | tf_op jit(solution)/shard_map/ppermute | solution.py:435
  5.1 13.3 %all-to-all-start = ((s32[32,1,128]{2,1,0:T(1,128)}), s32[32,1,128]{2,1,0:T(1,128)S(1)}, u32[]{:S(2)}, u32[]{:S(2)}) async-start(s32[32,1,128]{2,1,0:T(1,128)} %bitcast.8), calls=%async_computation | async-start | bytes 32768 | tf_op jit(solution)/shard_map/all_to_all | solution.py:429
  18.4 0.6 copy-start
  18.4 0.6 copy-start.1
  18.4 0.7 %copy-start.2 = (bf16[512,128]{1,0:T(8,128)(2,1)}, bf16[512,128]{1,0:T(8,128)(2,1)S(1)}, u32[]{:S(2)}) copy-start(bf16[512,128]{1,0:T(8,128)(2,1)S(1)} %collective-permute-done.1.rest_2_) | copy-start | bytes 393220
  18.4 0.7 %copy-start.3 = (bf16[512,128]{1,0:T(8,128)(2,1)}, bf16[512,128]{1,0:T(8,128)(2,1)S(1)}, u32[]{:S(2)}) copy-start(bf16[512,128]{1,0:T(8,128)(2,1)S(1)} %collective-permute-done.rest_1_) | copy-start | bytes 393220
